TPU v7x, 1024 devices: a whole 4x4x32 slice. The times are simulated.
1024 devices in a mesh: replica: 64 (over y, z_hi, x), fsdp: 16 (over z_lo, core).
Axes of the slice: x: 4, y: 4, z: 32 (z_hi: 4, z_lo: 8; z = z_hi * 8 + z_lo), core: 2. Of those that a mesh axis runs over, the one named last changes fastest.
Arguments:
- tokens: bfloat16 [131072, 8192], P(('replica', 'fsdp')), may hold values from -24 to 24
- cotangent: bfloat16 [131072, 512], P(('replica', 'fsdp')), may hold values from -0.125 to 0.125
- inner_weights: bfloat16 [64, 8192, 512], P('replica', 'fsdp'), may hold values from -16 to 16
- global_weights: bfloat16 [8192, 512], P('fsdp'), may hold values from -6 to 6
- momentum: float32 [8192, 512], P(('fsdp', 'replica')), may hold values from -4 to 4
- exponents: int32 [64, 256, 4], P('replica', 'fsdp'), may hold values from -1 to 2
Outputs:
- blended: bfloat16 [64, 8192, 512], P('replica', 'fsdp')
- global_next: bfloat16 [8192, 512], P('fsdp')
- momentum_next: float32 [8192, 512], P(('fsdp', 'replica'))
All inputs are finite; a program needn't handle non-finite values.
Results may differ from a plain program's by a relative error of at most 0.011.
Values may be sent and summed in bfloat16 or wider, within the bound.
A program may use at most 64 MiB of HBM per device.

v0:
```python
import jax
import jax.numpy as jnp
from jax import lax
from jax.sharding import PartitionSpec as P

SROWS = 32
SCOLS = 128


clip_level = 2.0
inner_rate = 0.5
outer_rate = 0.7
outer_momentum = 0.9
mixing = 0.5


def expand_scales(exponent_block):
    powers = jnp.exp2(exponent_block.astype(jnp.float32))
    return jnp.repeat(jnp.repeat(powers, SROWS, axis=0), SCOLS, axis=1)


def body(tokens, cotangent, inner_weights, global_weights, momentum, exponents):
    replicas = lax.axis_size("replica")
    shard_rows = momentum.shape[0]
    own_inner = inner_weights[0]
    contract = (((0,), (0,)), ((), ()))
    gradient = lax.psum_scatter(
        lax.dot_general(tokens, cotangent, contract, preferred_element_type=jnp.float32),
        "fsdp",
        scatter_dimension=0,
        tiled=True,
    )
    block_scale = expand_scales(exponents[0])
    pseudo_grad = global_weights.astype(jnp.float32) - own_inner.astype(jnp.float32)
    encoded = jnp.clip(pseudo_grad / block_scale, -clip_level, clip_level).astype(jnp.bfloat16)
    decoded = encoded.astype(jnp.float32) * block_scale
    summed = lax.psum_scatter(decoded, "replica", scatter_dimension=0, tiled=True)
    average = summed / replicas
    momentum_next = outer_momentum * momentum + average
    start_row = lax.axis_index("replica") * shard_rows
    own_global = lax.dynamic_slice_in_dim(global_weights, start_row, shard_rows, 0)
    global_part = (
        own_global.astype(jnp.float32) - outer_rate * (outer_momentum * momentum_next + average)
    ).astype(jnp.bfloat16)
    gathered = lax.all_gather(global_part, "replica", axis=0, tiled=True)
    gathered, momentum_next = (gathered, momentum_next)
    stepped = own_inner.astype(jnp.float32) - inner_rate * gradient
    blended = (mixing * stepped + (1.0 - mixing) * gathered.astype(jnp.float32)).astype(
        jnp.bfloat16
    )
    return (blended[None], gathered, momentum_next)


def solution(mesh):
    placed = (
        P(("replica", "fsdp"), None),
        P(("replica", "fsdp"), None),
        P("replica", "fsdp", None),
        P("fsdp", None),
        P(("fsdp", "replica"), None),
        P("replica", "fsdp", None),
    )
    return jax.shard_map(
        body,
        mesh=mesh,
        in_specs=placed,
        out_specs=(P("replica", "fsdp", None), P("fsdp", None), P(("fsdp", "replica"), None)),
        check_vma=False,
    )
```

profile of v0, /device:TPU:34, one launch (start us, length us, event | category | flops | bytes accessed | tf_op | source)
XLA Modules:
  0.0 946.4 jit_solution(4466822144742493479)
XLA Ops:
  7.2 0.0 copy-start
  7.2 0.0 reduce-scatter.5.cloned.1.call-start
  7.2 0.8 exponential_bitcast_fusion
  8.1 0.1 copy.9
  8.2 0.6 broadcast_in_dim.10
  8.8 0.0 copy-start.2
  8.8 2.5 bitcast_multiply_fusion
  11.3 0.0 reduce-scatter.5.cloned.1.call-update
  11.3 0.0 reduce-scatter.3.cloned.1.call-start
  11.4 0.0 copy-done
  11.4 0.0 copy-done.2
  11.4 8.1 fusion.7
  19.5 0.0 copy-start.3
  19.5 0.0 copy-start.1
  19.5 0.0 reduce-scatter.3.cloned.1.call-update
  19.5 597.1 %reduce-scatter.5.cloned.1.call-done = f32[8,512]{1,0:T(8,128)} async-done(((f32[512,512]{1,0:T(8,128)}), f32[8,512]{1,0:T(8,128)}) %reduce-scatter.5.cloned.1.call-update) | async-done | bytes 16400 | tf_op jit(solution)/shard_map/reduce_scatter | solution.py:37
  616.6 0.0 copy-done.3
  616.6 1.3 subtract_convert_fusion
  617.9 318.6 %all_gather.3 = bf16[512,512]{1,0:T(8,128)(2,1)S(1)} all-gather(bf16[8,512]{1,0:T(8,128)(2,1)S(1)} %get-tuple-element.3), channel_id=1, replica_groups=mesh['replica'=64,'fsdp'=16] {'replica'}, dimensions={0}, use_global_device_ids=true | all-gather | bytes 532480 | tf_op jit(solution)/shard_map/all_gather | solution.py:45
  936.5 0.0 reduce-scatter.3.cloned.1.call-done
  936.5 0.0 copy-done.1
  936.5 2.3 fusion.6
  938.7 0.8 copy.13
  (1 shorter events, 0.0 us)
Async XLA Ops:
  7.2 4.2 copy-start
  7.2 609.4 %reduce-scatter.5.cloned.1.call-start = ((), (), s32[]{:S(2)}) async-start(), calls=%async_computation.3 | async-start | bytes 1064960 | tf_op jit(solution)/shard_map/reduce_scatter | solution.py:37
  8.8 2.6 copy-start.2
  11.3 925.2 %reduce-scatter.3.cloned.1.call-start = ((), (), s32[]{:S(2)}) async-start(), calls=%async_computation.2 | async-start | bytes 17825792 | tf_op jit(solution)/shard_map/reduce_scatter | solution.py:27
  19.5 597.1 %copy-start.3 = (f32[8,512]{1,0:T(8,128)S(1)}, f32[8,512]{1,0:T(8,128)}, u32[]{:S(2)}) copy-start(f32[8,512]{1,0:T(8,128)} %param.10) | copy-start | bytes 49156
  19.5 917.0 %copy-start.1 = (bf16[1,512,512]{2,1,0:T(8,128)(2,1)S(1)}, bf16[1,512,512]{2,1,0:T(8,128)(2,1)}, u32[]{:S(2)}) copy-start(bf16[1,512,512]{2,1,0:T(8,128)(2,1)} %param.8) | copy-start | bytes 1572868
Sparse Core Ops, SparseCore 0:
  11.4 605.0 reduce-scatter.4
  620.4 186.8 reduce-scatter.2
where the time goes:
time: 947 us; the launch traced here: 946 us
  waiting for transfers between devices  597 us (63%)
  blocking collectives  319 us (34%)
  between operations  14.1 us (1%)
    reduce_scatter x1, waiting for transfers between devices, body(): lax.psum_scatter(decoded, 'replica', scatter_dimension=0, tiled=True)  597 us
    all_gather x1, blocking collectives, body(): gathered = lax.all_gather(global_part, 'replica', axis=0, tiled=True)  319 us
  transfers between devices with their start and end apart: 2, of which 1 were waited for; matrix products, arithmetic and copies ran while one was open for 1% of the time, Pallas kernels for 0%

commit v1 on v0

v1 whole, which is shorter than its diff:
```python
import functools

import jax
import jax.numpy as jnp
from jax import lax
from jax.experimental import pallas as pl
from jax.experimental.pallas import tpu as pltpu
from jax.sharding import PartitionSpec as P

MESH = pl.DeviceIdType.MESH
F32 = jnp.float32
BF16 = jnp.bfloat16

CHIPS = 8
TOK = 128
BLK = 512
QR = 128
HC = 256
NQ = BLK // QR
NH = BLK // HC
NC = NQ * NH
LAG = 4
STAGES = (8, 15, 21, 27, 32, 38)


def kernel(
    dims,
    replicas,
    tok,
    cot,
    inner,
    glob,
    mom,
    expo,
    blended,
    gnext,
    mnext,
    t_own,
    t_ext,
    c_own,
    c_ext,
    up_buf,
    dn_buf,
    acc,
    inner_v,
    glob_v,
    mom_v,
    out_v,
    gn_v,
    mn_v,
    dec,
    got1,
    part2,
    got2,
    part3,
    got3,
    gath,
    in_sem,
    tin_sem,
    sib_send,
    sib_recv,
    cx_send,
    cx_recv,
    tx_send,
    tx_recv,
    up_send,
    up_recv,
    dn_send,
    dn_recv,
    st_send,
    st_recv,
    out_sem,
):
    ny, nz, nx = dims
    r = lax.axis_index("replica")
    f = lax.axis_index("fsdp")
    i = f // 2
    c = lax.rem(f, 2)
    x = lax.rem(r, nx)
    z = lax.rem(r // nx, nz)
    y = r // (nx * nz)
    sib = (r, f + 1 - 2 * c)
    low_end, high_end = i == 0, i == CHIPS - 1
    is_end = low_end | high_end
    is_next = (i == 1) | (i == CHIPS - 2)
    paired = is_end | is_next
    mate_i = i + 1 - 2 * lax.rem(i, 2)
    mate = (r, 2 * mate_i + c)
    cross = (r, 2 * mate_i + 1 - c)
    above = (r, jnp.minimum(f + 2, 2 * CHIPS - 1))
    below = (r, jnp.maximum(f - 2, 0))

    def at(yy, zz, xx):
        return ((yy * nz + zz) * nx + xx, f)

    x_peers = [at(y, z, lax.rem(x + k, nx)) for k in range(1, nx)]
    y_peers = [at(lax.rem(y + k, ny), z, x) for k in range(1, ny)]
    z_peers = [at(y, lax.rem(z + k, nz), x) for k in range(1, nz)]

    def t_copy(d):
        return pltpu.make_async_copy(
            tok.at[:, pl.ds(pl.multiple_of((2 * d + c) * BLK, BLK), BLK)],
            t_own.at[0:TOK, pl.ds(pl.multiple_of(d * BLK, BLK), BLK)],
            tin_sem.at[d],
        )

    c_copy = pltpu.make_async_copy(cot, c_own.at[0:TOK], in_sem.at[0])
    i_copy = pltpu.make_async_copy(inner, inner_v, in_sem.at[1])
    g_copy = pltpu.make_async_copy(glob, glob_v, in_sem.at[2])
    m_copy = pltpu.make_async_copy(mom, mom_v, in_sem.at[3])
    i_copy.start()
    g_copy.start()
    c_copy.start()
    m_copy.start()

    @pl.loop(0, CHIPS)
    def _(d):
        t_copy(d).start()

    barrier = pltpu.get_barrier_semaphore()
    for peer in [sib] + x_peers + y_peers + z_peers:
        pl.semaphore_signal(barrier, 1, device_id=peer, device_id_type=MESH)

    @pl.when(i < CHIPS - 1)
    def _():
        pl.semaphore_signal(barrier, 1, device_id=above, device_id_type=MESH)

    @pl.when(i > 0)
    def _():
        pl.semaphore_signal(barrier, 1, device_id=below, device_id_type=MESH)

    @pl.when(paired)
    def _():
        pl.semaphore_signal(barrier, 1, device_id=cross, device_id_type=MESH)

    others = 1 + (nx - 1) + (ny - 1) + (nz - 1)
    pl.semaphore_wait(
        barrier,
        others + jnp.where(is_end, 1, 2) + jnp.where(paired, 1, 0),
    )

    def cx_copy():
        return pltpu.make_async_remote_copy(
            cot, c_ext.at[0:TOK], cx_send.at[0], cx_recv.at[0], device_id=mate, device_id_type=MESH
        )

    def cx_forward():
        return pltpu.make_async_remote_copy(
            c_ext.at[0:TOK],
            c_ext.at[TOK : 2 * TOK],
            cx_send.at[1],
            cx_recv.at[1],
            device_id=sib,
            device_id_type=MESH,
        )

    def tx_copy(k, q, other):
        d = jnp.where((i == 0) | (i == 1), CHIPS - 1 - k, k)
        src_c = (1 - c) if other else c
        return pltpu.make_async_remote_copy(
            tok.at[:, pl.ds(pl.multiple_of((2 * d + src_c) * BLK + q * QR, QR), QR)],
            t_ext.at[
                (TOK if other else 0) : (2 * TOK if other else TOK),
                pl.ds(pl.multiple_of(d * BLK + q * QR, QR), QR),
            ],
            tx_send.at[1 if other else 0],
            tx_recv.at[k * NQ + q, 1 if other else 0],
            device_id=cross if other else mate,
            device_id_type=MESH,
        )

    @pl.when(is_end)
    def _():
        cx_copy().start()

        @pl.loop(0, (CHIPS - 1) * NQ)
        def _(n):
            tx_copy(n // NQ, lax.rem(n, NQ), False).start()
            tx_copy(n // NQ, lax.rem(n, NQ), True).start()

    sc_copy = pltpu.make_async_remote_copy(
        cot,
        c_own.at[TOK : 2 * TOK],
        sib_send.at[CHIPS],
        sib_recv.at[CHIPS],
        device_id=sib,
        device_id_type=MESH,
    )

    def st_copy(d):
        return pltpu.make_async_remote_copy(
            tok.at[:, pl.ds(pl.multiple_of((2 * d + 1 - c) * BLK, BLK), BLK)],
            t_own.at[TOK : 2 * TOK, pl.ds(pl.multiple_of(d * BLK, BLK), BLK)],
            sib_send.at[d],
            sib_recv.at[d],
            device_id=sib,
            device_id_type=MESH,
        )

    sc_copy.start()

    @pl.loop(0, CHIPS)
    def _(d):
        st_copy(d).start()

    i_copy.wait()
    g_copy.wait()

    @pl.loop(0, BLK // 16)
    def _(t):
        rows = pl.ds(pl.multiple_of(t * 16, 16), 16)
        diff = glob_v[rows, :].astype(F32) - inner_v[rows, :].astype(F32)
        parts = []
        for b in range(4):
            e = expo[t // 2, b]
            lim = jnp.where(e < 0, 1.0, jnp.where(e == 0, 2.0, jnp.where(e == 1, 4.0, 8.0)))
            parts.append(jnp.clip(diff[:, b * 128 : (b + 1) * 128], -lim, lim))
        for half in range(2):
            rr = 2 * t + half
            packed = jnp.concatenate([p[8 * half : 8 * half + 8] for p in parts], axis=0)
            rx = lax.rem(rr, nx)
            rz = lax.rem(rr // nx, nz)
            ry = rr // (nx * nz)
            dec[rx, ry * nz + rz] = packed.astype(BF16)

    def stage_copy(stage, k, src, dst, peer):
        return pltpu.make_async_remote_copy(
            src, dst, st_send.at[stage, k], st_recv.at[stage, k], device_id=peer, device_id_type=MESH
        )

    def x_sum(k):
        return stage_copy(0, k, dec.at[lax.rem(x + k + 1, nx)], got1.at[k], x_peers[k])

    def y_sum(k):
        return stage_copy(1, k, part2.at[lax.rem(y + k + 1, ny)], got2.at[k], y_peers[k])

    def z_sum(k):
        return stage_copy(2, k, part3.at[lax.rem(z + k + 1, nz)], got3.at[k], z_peers[k])

    def z_gather(k, zz):
        ref = gath.at[x, y, zz]
        return stage_copy(3, k, ref, ref, z_peers[k])

    def y_gather(k, yy):
        ref = gath.at[x, yy]
        return stage_copy(4, k, ref, ref, y_peers[k])

    def x_gather(k, xx):
        ref = gath.at[xx]
        return stage_copy(5, k, ref, ref, x_peers[k])

    for k in range(nx - 1):
        x_sum(k).start()

    @pl.when(is_next)
    def _():
        cx_copy().wait_recv()
        cx_forward().start()

    c_copy.wait()

    @pl.loop(0, CHIPS)
    def _(d):
        t_copy(d).wait()
        st_copy(d).wait_recv()

    sc_copy.wait_recv()

    @pl.when(is_next)
    def _():
        cx_forward().wait_recv()

    def share(d, q, h, extra, k):
        cols = pl.ds(pl.multiple_of(d * BLK + q * QR, QR), QR)
        kv = pl.ds(pl.multiple_of(h * HC, HC), HC)
        contract = (((0,), (0,)), ((), ()))
        acc[...] = lax.dot_general(
            t_own[:, cols], c_own[:, kv], contract, preferred_element_type=F32
        )

        @pl.when(extra)
        def _():
            @pl.when(h == 0)
            def _():
                tx_copy(k, q, False).wait_recv()
                tx_copy(k, q, True).wait_recv()

            acc[...] += lax.dot_general(
                t_ext[:, cols], c_ext[:, kv], contract, preferred_element_type=F32
            )

    def up_copy(n):
        return pltpu.make_async_remote_copy(
            up_buf.at[n], up_buf.at[n], up_send.at[n // NC], up_recv.at[n], device_id=above, device_id_type=MESH
        )

    def dn_copy(n):
        return pltpu.make_async_remote_copy(
            dn_buf.at[n], dn_buf.at[n], dn_send.at[n // NC], dn_recv.at[n], device_id=below, device_id_type=MESH
        )

    ticks = (CHIPS - 2) * NC

    @pl.loop(0, ticks)
    def _(t):
        su = t - (i - 1) * LAG
        ku = su // NC

        @pl.when((i >= 1) & (su >= 0) & (su < (CHIPS - 1 - i) * NC))
        def _():
            d = CHIPS - 1 - ku
            p = lax.rem(su, NC)
            n = d * NC + p
            share(d, p // NH, lax.rem(p, NH), i == 1, ku)

            @pl.when(i > 1)
            def _():
                up_copy(n).wait_recv()
                up_buf[n] = (acc[...] + up_buf[n].astype(F32)).astype(BF16)

            @pl.when(i == 1)
            def _():
                up_buf[n] = acc[...].astype(BF16)

            up_copy(n).start()

        sd = t - (CHIPS - 2 - i) * LAG
        kd = sd // NC

        @pl.when((i <= CHIPS - 2) & (sd >= 0) & (sd < i * NC))
        def _():
            p = lax.rem(sd, NC)
            n = kd * NC + p
            share(kd, p // NH, lax.rem(p, NH), i == CHIPS - 2, kd)

            @pl.when(i < CHIPS - 2)
            def _():
                dn_copy(n).wait_recv()
                dn_buf[n] = (acc[...] + dn_buf[n].astype(F32)).astype(BF16)

            @pl.when(i == CHIPS - 2)
            def _():
                dn_buf[n] = acc[...].astype(BF16)

            dn_copy(n).start()

        @pl.when(t == STAGES[0])
        def _():
            for k in range(nx - 1):
                x_sum(k).wait_recv()

            @pl.loop(0, ny * nz)
            def _(g):
                total = dec[x, g].astype(F32)
                for k in range(nx - 1):
                    total += got1[k, g].astype(F32)
                part2[g // nz, lax.rem(g, nz)] = total.astype(BF16)

            for k in range(ny - 1):
                y_sum(k).start()

        @pl.when(t == STAGES[1])
        def _():
            for k in range(ny - 1):
                y_sum(k).wait_recv()
            for g in range(nz):
                total = part2[y, g].astype(F32)
                for k in range(ny - 1):
                    total += got2[k, g].astype(F32)
                part3[g] = total.astype(BF16)
            for k in range(nz - 1):
                z_sum(k).start()

        @pl.when(t == STAGES[2])
        def _():
            for k in range(nz - 1):
                z_sum(k).wait_recv()
            total = part3[z].astype(F32)
            for k in range(nz - 1):
                total += got3[k].astype(F32)
            average = total / replicas
            m_copy.wait()
            mom_now = mom_v[...]
            mom_p = jnp.concatenate([mom_now[:, b * 128 : (b + 1) * 128] for b in range(4)], axis=0)
            mom_next = 0.9 * mom_p + average
            own = glob_v[pl.ds(pl.multiple_of(r // 2 * 16, 16), 16), :].astype(F32)
            own = jnp.where(lax.rem(r, 2) == 0, own[0:8], own[8:16])
            own_p = jnp.concatenate([own[:, b * 128 : (b + 1) * 128] for b in range(4)], axis=0)
            gath[x, y, z] = (own_p - 0.7 * (0.9 * mom_next + average)).astype(BF16)
            for k in range(nz - 1):
                z_gather(k, z).start()
            for b in range(4):
                mn_v[:, b * 128 : (b + 1) * 128] = mom_next[8 * b : 8 * b + 8]
            pltpu.make_async_copy(mn_v, mnext, out_sem.at[0]).start()

        @pl.when(t == STAGES[3])
        def _():
            for k in range(nz - 1):
                z_gather(k, lax.rem(z + nz - k - 1, nz)).wait_recv()
            for k in range(ny - 1):
                y_gather(k, y).start()

        @pl.when(t == STAGES[4])
        def _():
            for k in range(ny - 1):
                y_gather(k, lax.rem(y + ny - k - 1, ny)).wait_recv()
            for k in range(nx - 1):
                x_gather(k, x).start()

        @pl.when(t == STAGES[5])
        def _():
            for k in range(nx - 1):
                x_gather(k, lax.rem(x + nx - k - 1, nx)).wait_recv()

            @pl.loop(0, BLK // 16)
            def _(n):
                halves = []
                for half in range(2):
                    rr = 2 * n + half
                    piece = gath[lax.rem(rr, nx), rr // (nx * nz), lax.rem(rr // nx, nz)].astype(F32)
                    halves.append(
                        jnp.concatenate([piece[8 * b : 8 * b + 8] for b in range(4)], axis=1)
                    )
                gn_v[pl.ds(pl.multiple_of(n * 16, 16), 16), :] = jnp.concatenate(
                    halves, axis=0
                ).astype(BF16)

            pltpu.make_async_copy(gn_v, gnext, out_sem.at[1]).start()

    def out_copy(q):
        rows = pl.ds(pl.multiple_of(q * QR, QR), QR)
        return pltpu.make_async_copy(out_v.at[rows], blended.at[rows], out_sem.at[2 + q])

    @pl.loop(0, NC)
    def _(p):
        q, h = p // NH, lax.rem(p, NH)
        n = i * NC + p
        share(i, q, h, is_next, CHIPS - 2)

        @pl.when(i <= CHIPS - 3)
        def _():
            dn_copy(n).wait_recv()
            acc[...] += dn_buf[n].astype(F32)

        @pl.when(i >= 2)
        def _():
            up_copy(n).wait_recv()
            acc[...] += up_buf[n].astype(F32)

        rows = pl.ds(pl.multiple_of(q * QR, QR), QR)
        kv = pl.ds(pl.multiple_of(h * HC, HC), HC)
        stepped = inner_v[rows, kv].astype(F32) - 0.5 * acc[...]
        out_v[rows, kv] = (0.5 * stepped + 0.5 * gn_v[rows, kv].astype(F32)).astype(BF16)

        @pl.when(h == NH - 1)
        def _():
            out_copy(q).start()

    sc_copy.wait_send()

    @pl.loop(0, CHIPS)
    def _(d):
        st_copy(d).wait_send()

    @pl.when(is_next)
    def _():
        cx_forward().wait_send()

    @pl.when(is_end)
    def _():
        cx_copy().wait_send()
        for other in range(2):
            whole = t_ext.at[0:TOK, 0 : (CHIPS - 1) * BLK]
            pltpu.make_async_copy(whole, whole, tx_send.at[other]).wait()

    def wait_block(buf, sem, d):
        whole = buf.at[pl.ds(d * NC, NC)]
        pltpu.make_async_copy(whole, whole, sem.at[d]).wait()

    @pl.loop(0, CHIPS)
    def _(d):
        @pl.when((i >= 1) & (d > i))
        def _():
            wait_block(up_buf, up_send, d)

        @pl.when((i <= CHIPS - 2) & (d < i))
        def _():
            wait_block(dn_buf, dn_send, d)

    for k in range(nx - 1):
        x_sum(k).wait_send()
        x_gather(k, x).wait_send()
    for k in range(ny - 1):
        y_sum(k).wait_send()
        y_gather(k, y).wait_send()
    for k in range(nz - 1):
        z_sum(k).wait_send()
        z_gather(k, z).wait_send()
    pltpu.make_async_copy(mn_v, mnext, out_sem.at[0]).wait()
    pltpu.make_async_copy(gn_v, gnext, out_sem.at[1]).wait()
    for q in range(NQ):
        out_copy(q).wait()


def body(dims, tokens, cotangent, inner_weights, global_weights, momentum, exponents):
    ny, nz, nx = dims
    replicas = ny * nz * nx
    anywhere = pl.BlockSpec(memory_space=pl.ANY)
    sem = pltpu.SemaphoreType.DMA
    blended, gnext, mnext = pl.pallas_call(
        functools.partial(kernel, dims, replicas),
        out_shape=(
            jax.ShapeDtypeStruct((BLK, BLK), BF16),
            jax.ShapeDtypeStruct((BLK, BLK), BF16),
            jax.ShapeDtypeStruct((8, BLK), F32),
        ),
        in_specs=[anywhere] * 5 + [pl.BlockSpec(memory_space=pltpu.SMEM)],
        out_specs=(anywhere,) * 3,
        scratch_shapes=[
            pltpu.VMEM((2 * TOK, CHIPS * BLK), BF16),
            pltpu.VMEM((2 * TOK, CHIPS * BLK), BF16),
            pltpu.VMEM((2 * TOK, BLK), BF16),
            pltpu.VMEM((2 * TOK, BLK), BF16),
            pltpu.VMEM((CHIPS * NC, QR, HC), BF16),
            pltpu.VMEM((CHIPS * NC, QR, HC), BF16),
            pltpu.VMEM((QR, HC), F32),
            pltpu.VMEM((BLK, BLK), BF16),
            pltpu.VMEM((BLK, BLK), BF16),
            pltpu.VMEM((8, BLK), F32),
            pltpu.VMEM((BLK, BLK), BF16),
            pltpu.VMEM((BLK, BLK), BF16),
            pltpu.VMEM((8, BLK), F32),
            pltpu.VMEM((nx, 64 // nx, 32, 128), BF16),
            pltpu.VMEM((3, ny * nz, 32, 128), BF16),
            pltpu.VMEM((ny, nz, 32, 128), BF16),
            pltpu.VMEM((3, nz, 32, 128), BF16),
            pltpu.VMEM((nz, 32, 128), BF16),
            pltpu.VMEM((3, 32, 128), BF16),
            pltpu.VMEM((nx, 64 // (nx * nz), nz, 32, 128), BF16),
            sem((4,)),
            sem((CHIPS,)),
            sem((CHIPS + 1,)),
            sem((CHIPS + 1,)),
            sem((2,)),
            sem((2,)),
            sem((2,)),
            sem(((CHIPS - 1) * NQ, 2)),
            sem((CHIPS,)),
            sem((CHIPS * NC,)),
            sem((CHIPS,)),
            sem((CHIPS * NC,)),
            sem((6, 3)),
            sem((6, 3)),
            sem((2 + NQ,)),
        ],
        compiler_params=pltpu.CompilerParams(
            collective_id=0, has_side_effects=True, vmem_limit_bytes=48 << 20
        ),
    )(tokens, cotangent, inner_weights[0], global_weights, momentum, exponents[0])
    return blended[None], gnext, mnext


def solution(mesh):
    return jax.shard_map(
        functools.partial(body, (4, 4, 4)),
        mesh=mesh,
        in_specs=(
            P(("replica", "fsdp"), None),
            P(("replica", "fsdp"), None),
            P("replica", "fsdp", None),
            P("fsdp", None),
            P(("fsdp", "replica"), None),
            P("replica", "fsdp", None),
        ),
        out_specs=(P("replica", "fsdp", None), P("fsdp", None), P(("fsdp", "replica"), None)),
        check_vma=False,
    )
```

time: 947 us -> 127 us (0.13)
  the two profiles are of different devices: /device:TPU:34 before, /device:TPU:8 now
where the time goes in v1:
time: 127 us
  Pallas kernels  118 us (93%)
  local copies, waits for them, and re-layouts  8.25 us (6%)
    pallas_call x1, Pallas kernels, body(): pl.pallas_call(functools.partial(kernel, dims, replicas), out_shape=(jax....  118 us
    unnamed x13, local copies, waits for them, and re-layouts  7.49 us

profile of v1, /device:TPU:8, one launch (start us, length us, event | category | flops | bytes accessed | tf_op | source)
XLA Modules:
  0.0 126.7 jit_solution(2860900443204991745)
XLA Ops:
  0.6 0.8 copy.9.expo
  1.4 0.0 copy-start
  1.4 1.6 %copy-done = bf16[128,8192]{1,0:T(8,128)(2,1)S(1)} copy-done((bf16[128,8192]{1,0:T(8,128)(2,1)S(1)}, bf16[128,8192]{1,0:T(8,128)(2,1)}, u32[]{:S(2)}) %copy-start) | copy-done | bytes 2097176
  3.0 0.0 copy-start.1
  3.0 1.0 copy-done.1
  4.0 0.0 copy-start.2
  4.0 1.0 copy-done.2
  5.1 0.0 copy-start.3
  5.1 0.9 copy-done.3
  6.0 0.0 copy-start.4
  6.0 0.7 copy-done.4
  6.7 117.8 %shard_map.85 = (bf16[512,512]{1,0:T(8,128)(2,1)S(1)}, bf16[512,512]{1,0:T(8,128)(2,1)S(1)}, f32[8,512]{1,0:T(8,128)S(1)}) custom-call(bf16[128,8192]{1,0:T(8,128)(2,1)S(1)} %copy-done, bf16[128,512]{1,0:T(8,128)(2,1)S(1)} %copy-done.3, bf16[512,512]{1,0:T(8,128)(2,1)S(1)} %bitcast.3, bf16[512,512]{1,0:T(8,128)(2,1)S(1)} %copy-done.2, ...), custom_call_target="tpu_custom_call" | custom-call | tf_op jit(solution)/shard_map/pallas_call | solution.py:510
  124.5 0.8 copy.13
  125.3 0.8 copy.14
  126.1 0.6 copy.15
Async XLA Ops:
  1.4 1.6 %copy-start = (bf16[128,8192]{1,0:T(8,128)(2,1)S(1)}, bf16[128,8192]{1,0:T(8,128)(2,1)}, u32[]{:S(2)}) copy-start(bf16[128,8192]{1,0:T(8,128)(2,1)} %tok.1) | copy-start | bytes 6291460
  3.0 1.0 copy-start.1
  4.0 1.0 copy-start.2
  5.1 0.9 copy-start.3
  6.0 0.7 copy-start.4

commit v2 on v1

--- a/solution.py
+++ b/solution.py
@@ -15,12 +15,22 @@
 TOK = 128
 BLK = 512
 QR = 128
-HC = 256
+HC = 512
 NQ = BLK // QR
 NH = BLK // HC
 NC = NQ * NH
-LAG = 4
-STAGES = (8, 15, 21, 27, 32, 38)
+LAG = 3
+DECODE = 1
+STAGES = (
+    (4, 4, 4, 4),
+    (7, 7, 6, 6),
+    (12, 10, 9, 10),
+    (15, 13, 12, 12),
+    (17, 15, 14, 15),
+    (19, 18, 17, 17),
+    (21, 19, 18, 19),
+    (23, 22, 21, 22),
+)
 
 
 def kernel(
@@ -32,9 +42,9 @@
     glob,
     mom,
     expo,
-    blended,
-    gnext,
-    mnext,
+    out_v,
+    gn_v,
+    mn_v,
     t_own,
     t_ext,
     c_own,
@@ -45,14 +55,12 @@
     inner_v,
     glob_v,
     mom_v,
-    out_v,
-    gn_v,
-    mn_v,
     dec,
     got1,
     part2,
     got2,
     part3,
+    far3,
     got3,
     gath,
     in_sem,
@@ -69,7 +77,7 @@
     dn_recv,
     st_send,
     st_recv,
-    out_sem,
+    tok_go,
 ):
     ny, nz, nx = dims
     r = lax.axis_index("replica")
@@ -95,7 +103,6 @@
 
     x_peers = [at(y, z, lax.rem(x + k, nx)) for k in range(1, nx)]
     y_peers = [at(lax.rem(y + k, ny), z, x) for k in range(1, ny)]
-    z_peers = [at(y, lax.rem(z + k, nz), x) for k in range(1, nz)]
 
     def t_copy(d):
         return pltpu.make_async_copy(
@@ -117,66 +124,118 @@
     def _(d):
         t_copy(d).start()
 
+    root = min(2, nz - 1)
+    leader_i = jnp.where((z == root) & (nz > 1), CHIPS // 2 - 1, CHIPS - 1)
+    leader = i == leader_i
+    line = [(r, lax.rem(f + 2 * k, 2 * CHIPS)) for k in range(1, CHIPS)]
+
+    def at_z(zz):
+        return at(y, zz, x)
+
+    def signal(semaphore, peer):
+        pl.semaphore_signal(semaphore, 1, device_id=peer, device_id_type=MESH)
+
     barrier = pltpu.get_barrier_semaphore()
-    for peer in [sib] + x_peers + y_peers + z_peers:
-        pl.semaphore_signal(barrier, 1, device_id=peer, device_id_type=MESH)
+    for peer in [sib] + x_peers + y_peers:
+        signal(barrier, peer)
 
     @pl.when(i < CHIPS - 1)
     def _():
-        pl.semaphore_signal(barrier, 1, device_id=above, device_id_type=MESH)
+        signal(barrier, above)
 
     @pl.when(i > 0)
     def _():
-        pl.semaphore_signal(barrier, 1, device_id=below, device_id_type=MESH)
+        signal(barrier, below)
 
     @pl.when(paired)
     def _():
-        pl.semaphore_signal(barrier, 1, device_id=cross, device_id_type=MESH)
-
-    others = 1 + (nx - 1) + (ny - 1) + (nz - 1)
-    pl.semaphore_wait(
-        barrier,
-        others + jnp.where(is_end, 1, 2) + jnp.where(paired, 1, 0),
-    )
-
-    def cx_copy():
+        signal(barrier, cross)
+
+    @pl.when((i < leader_i - 1) | (i > leader_i + 1))
+    def _():
+        signal(barrier, (r, 2 * leader_i + c))
+
+    near = jnp.where(leader, CHIPS - 1 + jnp.where(z == root, nz - 1, 0), jnp.where(is_end, 1, 2))
+    pl.semaphore_wait(barrier, 1 + (nx - 1) + (ny - 1) + near + jnp.where(paired, 1, 0))
+
+    if nz > 1:
+
+        @pl.when(leader & (z != root))
+        def _():
+            signal(barrier, (at_z(root)[0], 2 * (CHIPS // 2 - 1) + c))
+
+    def all_groups():
+        @pl.when(z == root)
+        def _():
+            for k in range(1, nz):
+                signal(tok_go, (at_z(lax.rem(z + k, nz))[0], 2 * (CHIPS - 1) + c))
+
+        @pl.when(z != root)
+        def _():
+            pl.semaphore_wait(tok_go, 1)
+
+        for peer in line:
+            signal(tok_go, peer)
+
+    def cx_copy(h):
+        cols = slice(h * 256, h * 256 + 256)
         return pltpu.make_async_remote_copy(
-            cot, c_ext.at[0:TOK], cx_send.at[0], cx_recv.at[0], device_id=mate, device_id_type=MESH
-        )
-
-    def cx_forward():
+            cot.at[:, cols],
+            c_ext.at[0:TOK, cols],
+            cx_send.at[h],
+            cx_recv.at[h],
+            device_id=mate,
+            device_id_type=MESH,
+        )
+
+    def cx_forward(h):
+        cols = slice(h * 256, h * 256 + 256)
         return pltpu.make_async_remote_copy(
-            c_ext.at[0:TOK],
-            c_ext.at[TOK : 2 * TOK],
-            cx_send.at[1],
-            cx_recv.at[1],
+            c_ext.at[0:TOK, cols],
+            c_ext.at[TOK : 2 * TOK, cols],
+            cx_send.at[2 + h],
+            cx_recv.at[2 + h],
             device_id=sib,
             device_id_type=MESH,
         )
 
-    def tx_copy(k, q, other):
+    def tx_copy(k, q, width, n, other):
         d = jnp.where((i == 0) | (i == 1), CHIPS - 1 - k, k)
         src_c = (1 - c) if other else c
         return pltpu.make_async_remote_copy(
-            tok.at[:, pl.ds(pl.multiple_of((2 * d + src_c) * BLK + q * QR, QR), QR)],
+            tok.at[:, pl.ds(pl.multiple_of((2 * d + src_c) * BLK + q * QR, QR), width)],
             t_ext.at[
                 (TOK if other else 0) : (2 * TOK if other else TOK),
-                pl.ds(pl.multiple_of(d * BLK + q * QR, QR), QR),
+                pl.ds(pl.multiple_of(d * BLK + q * QR, QR), width),
             ],
             tx_send.at[1 if other else 0],
-            tx_recv.at[k * NQ + q, 1 if other else 0],
+            tx_recv.at[n, 1 if other else 0],
             device_id=cross if other else mate,
             device_id_type=MESH,
         )
 
+    def tx_part(q, other):
+        return tx_copy(0, q, QR, q, other)
+
+    def tx_whole(k, other):
+        return tx_copy(k, 0, BLK, NQ - 1 + k, other)
+
     @pl.when(is_end)
     def _():
-        cx_copy().start()
-
-        @pl.loop(0, (CHIPS - 1) * NQ)
-        def _(n):
-            tx_copy(n // NQ, lax.rem(n, NQ), False).start()
-            tx_copy(n // NQ, lax.rem(n, NQ), True).start()
+        cx_copy(0).start()
+        tx_part(0, False).start()
+        tx_part(0, True).start()
+        cx_copy(1).start()
+
+        @pl.loop(1, NQ)
+        def _(q):
+            tx_part(q, False).start()
+            tx_part(q, True).start()
+
+        @pl.loop(1, CHIPS - 1)
+        def _(k):
+            tx_whole(k, False).start()
+            tx_whole(k, True).start()
 
     sc_copy = pltpu.make_async_remote_copy(
         cot,
@@ -203,26 +262,6 @@
     def _(d):
         st_copy(d).start()
 
-    i_copy.wait()
-    g_copy.wait()
-
-    @pl.loop(0, BLK // 16)
-    def _(t):
-        rows = pl.ds(pl.multiple_of(t * 16, 16), 16)
-        diff = glob_v[rows, :].astype(F32) - inner_v[rows, :].astype(F32)
-        parts = []
-        for b in range(4):
-            e = expo[t // 2, b]
-            lim = jnp.where(e < 0, 1.0, jnp.where(e == 0, 2.0, jnp.where(e == 1, 4.0, 8.0)))
-            parts.append(jnp.clip(diff[:, b * 128 : (b + 1) * 128], -lim, lim))
-        for half in range(2):
-            rr = 2 * t + half
-            packed = jnp.concatenate([p[8 * half : 8 * half + 8] for p in parts], axis=0)
-            rx = lax.rem(rr, nx)
-            rz = lax.rem(rr // nx, nz)
-            ry = rr // (nx * nz)
-            dec[rx, ry * nz + rz] = packed.astype(BF16)
-
     def stage_copy(stage, k, src, dst, peer):
         return pltpu.make_async_remote_copy(
             src, dst, st_send.at[stage, k], st_recv.at[stage, k], device_id=peer, device_id_type=MESH
@@ -234,41 +273,52 @@
     def y_sum(k):
         return stage_copy(1, k, part2.at[lax.rem(y + k + 1, ny)], got2.at[k], y_peers[k])
 
+    z_next = [at_z(lax.rem(z + 1, nz)), at_z(lax.rem(z + nz - 1, nz))]
+    half = [slice(0, 16), slice(16, 32)]
+
+    def z_far(k):
+        src = part3.at[lax.rem(z + 2, nz), half[k]]
+        return stage_copy(2, k, src, far3.at[k], z_next[k])
+
     def z_sum(k):
-        return stage_copy(2, k, part3.at[lax.rem(z + k + 1, nz)], got3.at[k], z_peers[k])
+        src = part3.at[lax.rem(z + (1, nz - 1)[k], nz)]
+        return stage_copy(3, k, src, got3.at[k], z_next[k])
 
     def z_gather(k, zz):
         ref = gath.at[x, y, zz]
-        return stage_copy(3, k, ref, ref, z_peers[k])
+        return stage_copy(4, k, ref, ref, z_next[k])
+
+    def z_pass(k, zz):
+        ref = gath.at[x, y, zz, half[k]]
+        return stage_copy(5, k, ref, ref, z_next[k])
 
     def y_gather(k, yy):
         ref = gath.at[x, yy]
-        return stage_copy(4, k, ref, ref, y_peers[k])
+        return stage_copy(6, k, ref, ref, y_peers[k])
 
     def x_gather(k, xx):
         ref = gath.at[xx]
-        return stage_copy(5, k, ref, ref, x_peers[k])
-
-    for k in range(nx - 1):
-        x_sum(k).start()
+        return stage_copy(7, k, ref, ref, x_peers[k])
 
     @pl.when(is_next)
     def _():
-        cx_copy().wait_recv()
-        cx_forward().start()
-
-    c_copy.wait()
-
-    @pl.loop(0, CHIPS)
-    def _(d):
+        for h in range(2):
+            cx_copy(h).wait_recv()
+            cx_forward(h).start()
+
+    def t_wait(d):
         t_copy(d).wait()
         st_copy(d).wait_recv()
 
+    c_copy.wait()
     sc_copy.wait_recv()
+    t_wait(CHIPS - 1)
+    t_wait(0)
 
     @pl.when(is_next)
     def _():
-        cx_forward().wait_recv()
+        for h in range(2):
+            cx_forward(h).wait_recv()
 
     def share(d, q, h, extra, k):
         cols = pl.ds(pl.multiple_of(d * BLK + q * QR, QR), QR)
@@ -280,10 +330,15 @@
 
         @pl.when(extra)
         def _():
-            @pl.when(h == 0)
+            @pl.when((h == 0) & (k == 0))
             def _():
-                tx_copy(k, q, False).wait_recv()
-                tx_copy(k, q, True).wait_recv()
+                tx_part(q, False).wait_recv()
+                tx_part(q, True).wait_recv()
+
+            @pl.when((h == 0) & (q == 0) & (k > 0))
+            def _():
+                tx_whole(k, False).wait_recv()
+                tx_whole(k, True).wait_recv()
 
             acc[...] += lax.dot_general(
                 t_ext[:, cols], c_ext[:, kv], contract, preferred_element_type=F32
@@ -298,6 +353,12 @@
         return pltpu.make_async_remote_copy(
             dn_buf.at[n], dn_buf.at[n], dn_send.at[n // NC], dn_recv.at[n], device_id=below, device_id_type=MESH
         )
+
+    def due(stage, t):
+        when = STAGES[stage][0]
+        for group in range(1, 4):
+            when = jnp.where(z == group, STAGES[stage][group], when)
+        return t == when
 
     ticks = (CHIPS - 2) * NC
 
@@ -344,7 +405,42 @@
 
             dn_copy(n).start()
 
-        @pl.when(t == STAGES[0])
+        @pl.when(t == DECODE)
+        def _():
+            @pl.loop(1, CHIPS - 1)
+            def _(d):
+                t_wait(d)
+
+            i_copy.wait()
+            g_copy.wait()
+
+            @pl.loop(0, BLK // 16)
+            def _(t):
+                rows = pl.ds(pl.multiple_of(t * 16, 16), 16)
+                diff = glob_v[rows, :].astype(F32) - inner_v[rows, :].astype(F32)
+                parts = []
+                for b in range(4):
+                    e = expo[b, t // 2]
+                    lim = jnp.where(e < 0, 1.0, jnp.where(e == 0, 2.0, jnp.where(e == 1, 4.0, 8.0)))
+                    parts.append(jnp.clip(diff[:, b * 128 : (b + 1) * 128], -lim, lim))
+                for half in range(2):
+                    rr = 2 * t + half
+                    packed = jnp.concatenate([p[8 * half : 8 * half + 8] for p in parts], axis=0)
+                    rx = lax.rem(rr, nx)
+                    rz = lax.rem(rr // nx, nz)
+                    ry = rr // (nx * nz)
+                    dec[rx, ry * nz + rz] = packed.astype(BF16)
+
+            for k in range(nx - 1):
+                x_sum(k).start()
+
+            if nz > 1:
+
+                @pl.when(leader)
+                def _():
+                    all_groups()
+
+        @pl.when(due(0, t))
         def _():
             for k in range(nx - 1):
                 x_sum(k).wait_recv()
@@ -354,30 +450,47 @@
                 total = dec[x, g].astype(F32)
                 for k in range(nx - 1):
                     total += got1[k, g].astype(F32)
-                part2[g // nz, lax.rem(g, nz)] = total.astype(BF16)
+                part2[g // nz, lax.rem(g, nz)] = total
 
             for k in range(ny - 1):
                 y_sum(k).start()
 
-        @pl.when(t == STAGES[1])
+        @pl.when(due(1, t))
         def _():
             for k in range(ny - 1):
                 y_sum(k).wait_recv()
             for g in range(nz):
-                total = part2[y, g].astype(F32)
+                total = part2[y, g]
                 for k in range(ny - 1):
-                    total += got2[k, g].astype(F32)
-                part3[g] = total.astype(BF16)
-            for k in range(nz - 1):
-                z_sum(k).start()
-
-        @pl.when(t == STAGES[2])
-        def _():
-            for k in range(nz - 1):
-                z_sum(k).wait_recv()
-            total = part3[z].astype(F32)
-            for k in range(nz - 1):
-                total += got3[k].astype(F32)
+                    total += got2[k, g]
+                part3[g] = total
+
+            if nz > 1:
+
+                @pl.when(jnp.logical_not(leader))
+                def _():
+                    pl.semaphore_wait(tok_go, 1)
+
+                for k in range(2):
+                    z_far(k).start()
+
+        @pl.when(due(2, t))
+        def _():
+            if nz > 1:
+                for k in range(2):
+                    z_far(k).wait_recv()
+                    to = lax.rem(z + (1, nz - 1)[k], nz)
+                    part3[to, half[k]] += far3[k]
+                for k in range(2):
+                    z_sum(k).start()
+
+        @pl.when(due(3, t))
+        def _():
+            total = part3[z]
+            if nz > 1:
+                for k in range(2):
+                    z_sum(k).wait_recv()
+                    total += got3[k]
             average = total / replicas
             m_copy.wait()
             mom_now = mom_v[...]
@@ -387,27 +500,36 @@
             own = jnp.where(lax.rem(r, 2) == 0, own[0:8], own[8:16])
             own_p = jnp.concatenate([own[:, b * 128 : (b + 1) * 128] for b in range(4)], axis=0)
             gath[x, y, z] = (own_p - 0.7 * (0.9 * mom_next + average)).astype(BF16)
-            for k in range(nz - 1):
-                z_gather(k, z).start()
+            if nz > 1:
+                for k in range(2):
+                    z_gather(k, z).start()
             for b in range(4):
                 mn_v[:, b * 128 : (b + 1) * 128] = mom_next[8 * b : 8 * b + 8]
-            pltpu.make_async_copy(mn_v, mnext, out_sem.at[0]).start()
-
-        @pl.when(t == STAGES[3])
-        def _():
-            for k in range(nz - 1):
-                z_gather(k, lax.rem(z + nz - k - 1, nz)).wait_recv()
+
+        @pl.when(due(4, t))
+        def _():
+            if nz > 1:
+                for k in range(2):
+                    before = lax.rem(z + (nz - 1, 1)[k], nz)
+                    z_gather(k, before).wait_recv()
+                    z_pass(k, before).start()
+
+        @pl.when(due(5, t))
+        def _():
+            if nz > 1:
+                for k in range(2):
+                    z_pass(k, lax.rem(z + 2, nz)).wait_recv()
             for k in range(ny - 1):
                 y_gather(k, y).start()
 
-        @pl.when(t == STAGES[4])
+        @pl.when(due(6, t))
         def _():
             for k in range(ny - 1):
                 y_gather(k, lax.rem(y + ny - k - 1, ny)).wait_recv()
             for k in range(nx - 1):
                 x_gather(k, x).start()
 
-        @pl.when(t == STAGES[5])
+        @pl.when(due(7, t))
         def _():
             for k in range(nx - 1):
                 x_gather(k, lax.rem(x + nx - k - 1, nx)).wait_recv()
@@ -425,11 +547,6 @@
                     halves, axis=0
                 ).astype(BF16)
 
-            pltpu.make_async_copy(gn_v, gnext, out_sem.at[1]).start()
-
-    def out_copy(q):
-        rows = pl.ds(pl.multiple_of(q * QR, QR), QR)
-        return pltpu.make_async_copy(out_v.at[rows], blended.at[rows], out_sem.at[2 + q])
 
     @pl.loop(0, NC)
     def _(p):
@@ -452,10 +569,6 @@
         stepped = inner_v[rows, kv].astype(F32) - 0.5 * acc[...]
         out_v[rows, kv] = (0.5 * stepped + 0.5 * gn_v[rows, kv].astype(F32)).astype(BF16)
 
-        @pl.when(h == NH - 1)
-        def _():
-            out_copy(q).start()
-
     sc_copy.wait_send()
 
     @pl.loop(0, CHIPS)
@@ -464,11 +577,13 @@
 
     @pl.when(is_next)
     def _():
-        cx_forward().wait_send()
+        for h in range(2):
+            cx_forward(h).wait_send()
 
     @pl.when(is_end)
     def _():
-        cx_copy().wait_send()
+        for h in range(2):
+            cx_copy(h).wait_send()
         for other in range(2):
             whole = t_ext.at[0:TOK, 0 : (CHIPS - 1) * BLK]
             pltpu.make_async_copy(whole, whole, tx_send.at[other]).wait()
@@ -493,13 +608,23 @@
     for k in range(ny - 1):
         y_sum(k).wait_send()
         y_gather(k, y).wait_send()
-    for k in range(nz - 1):
-        z_sum(k).wait_send()
-        z_gather(k, z).wait_send()
-    pltpu.make_async_copy(mn_v, mnext, out_sem.at[0]).wait()
-    pltpu.make_async_copy(gn_v, gnext, out_sem.at[1]).wait()
-    for q in range(NQ):
-        out_copy(q).wait()
+    if nz > 1:
+        for k in range(2):
+            z_far(k).wait_send()
+            z_sum(k).wait_send()
+            z_gather(k, z).wait_send()
+            z_pass(k, lax.rem(z + (nz - 1, 1)[k], nz)).wait_send()
+
+
+def store(a, b, c, a_out, b_out, c_out, sems):
+    copies = [
+        pltpu.make_async_copy(src, dst, sems.at[k])
+        for k, (src, dst) in enumerate(((a, a_out), (b, b_out), (c, c_out)))
+    ]
+    for copy in copies:
+        copy.start()
+    for copy in copies:
+        copy.wait()
 
 
 def body(dims, tokens, cotangent, inner_weights, global_weights, momentum, exponents):
@@ -510,12 +635,12 @@
     blended, gnext, mnext = pl.pallas_call(
         functools.partial(kernel, dims, replicas),
         out_shape=(
-            jax.ShapeDtypeStruct((BLK, BLK), BF16),
-            jax.ShapeDtypeStruct((BLK, BLK), BF16),
-            jax.ShapeDtypeStruct((8, BLK), F32),
+            pltpu.VMEM((BLK, BLK), BF16),
+            pltpu.VMEM((BLK, BLK), BF16),
+            pltpu.VMEM((8, BLK), F32),
         ),
         in_specs=[anywhere] * 5 + [pl.BlockSpec(memory_space=pltpu.SMEM)],
-        out_specs=(anywhere,) * 3,
+        out_specs=(pl.BlockSpec(memory_space=pltpu.VMEM),) * 3,
         scratch_shapes=[
             pltpu.VMEM((2 * TOK, CHIPS * BLK), BF16),
             pltpu.VMEM((2 * TOK, CHIPS * BLK), BF16),
@@ -527,36 +652,46 @@
             pltpu.VMEM((BLK, BLK), BF16),
             pltpu.VMEM((BLK, BLK), BF16),
             pltpu.VMEM((8, BLK), F32),
-            pltpu.VMEM((BLK, BLK), BF16),
-            pltpu.VMEM((BLK, BLK), BF16),
-            pltpu.VMEM((8, BLK), F32),
             pltpu.VMEM((nx, 64 // nx, 32, 128), BF16),
             pltpu.VMEM((3, ny * nz, 32, 128), BF16),
-            pltpu.VMEM((ny, nz, 32, 128), BF16),
-            pltpu.VMEM((3, nz, 32, 128), BF16),
-            pltpu.VMEM((nz, 32, 128), BF16),
-            pltpu.VMEM((3, 32, 128), BF16),
+            pltpu.VMEM((ny, nz, 32, 128), F32),
+            pltpu.VMEM((3, nz, 32, 128), F32),
+            pltpu.VMEM((nz, 32, 128), F32),
+            pltpu.VMEM((2, 16, 128), F32),
+            pltpu.VMEM((2, 32, 128), F32),
             pltpu.VMEM((nx, 64 // (nx * nz), nz, 32, 128), BF16),
             sem((4,)),
             sem((CHIPS,)),
             sem((CHIPS + 1,)),
             sem((CHIPS + 1,)),
+            sem((4,)),
+            sem((4,)),
             sem((2,)),
-            sem((2,)),
-            sem((2,)),
-            sem(((CHIPS - 1) * NQ, 2)),
+            sem((NQ + CHIPS - 2, 2)),
             sem((CHIPS,)),
             sem((CHIPS * NC,)),
             sem((CHIPS,)),
             sem((CHIPS * NC,)),
-            sem((6, 3)),
-            sem((6, 3)),
-            sem((2 + NQ,)),
+            sem((8, 3)),
+            sem((8, 3)),
+            pltpu.SemaphoreType.REGULAR,
         ],
         compiler_params=pltpu.CompilerParams(
-            collective_id=0, has_side_effects=True, vmem_limit_bytes=48 << 20
+            collective_id=0, has_side_effects=True, vmem_limit_bytes=62 << 20
         ),
-    )(tokens, cotangent, inner_weights[0], global_weights, momentum, exponents[0])
+    )(tokens, cotangent, inner_weights[0], global_weights, momentum, jnp.swapaxes(exponents[0], 0, 1))
+    blended, gnext, mnext = pl.pallas_call(
+        store,
+        out_shape=(
+            jax.ShapeDtypeStruct((BLK, BLK), BF16),
+            jax.ShapeDtypeStruct((BLK, BLK), BF16),
+            jax.ShapeDtypeStruct((8, BLK), F32),
+        ),
+        in_specs=[anywhere] * 3,
+        out_specs=(anywhere,) * 3,
+        scratch_shapes=[sem((3,))],
+        compiler_params=pltpu.CompilerParams(vmem_limit_bytes=1 << 20),
+    )(blended, gnext, mnext)
     return blended[None], gnext, mnext
 
 

time: 127 us -> 111 us (0.87)
  the two profiles are of different devices: /device:TPU:8 before, /device:TPU:4 now
where the time goes in v2:
time: 111 us
  Pallas kernels  111 us (100%)
    pallas_call x1, Pallas kernels, body(): pl.pallas_call(functools.partial(kernel, dims, replicas), out_shape=(pltp...  110 us

profile of v2, /device:TPU:4, one launch (start us, length us, event | category | flops | bytes accessed | tf_op | source)
XLA Modules:
  0.0 111.2 jit_solution(14313922946393908507)
XLA Ops:
  0.6 109.5 %shard_map.85 = (bf16[512,512]{1,0:T(8,128)(2,1)S(1)}, bf16[512,512]{1,0:T(8,128)(2,1)S(1)}, f32[8,512]{1,0:T(8,128)S(1)}) custom-call(bf16[128,8192]{1,0:T(8,128)(2,1)} %tok.1, bf16[128,512]{1,0:T(8,128)(2,1)} %cot.1, bf16[512,512]{1,0:T(8,128)(2,1)} %bitcast.5, bf16[512,512]{1,0:T(8,128)(2,1)} %glob.1, f32[8,512]{1,0:T(8,128)} %mom.1, s32[4,16]{1,0:T(4,128)} %bitcast.6), custom_call_target="tpu_custom_call" | custom-call | tf_op jit(solution)/shard_map/pallas_call | solution.py:635
  110.2 1.0 shard_map.86

commit v3 on v2

--- a/solution.py
+++ b/solution.py
@@ -21,15 +21,15 @@
 NC = NQ * NH
 LAG = 3
 DECODE = 1
+DEPTH = 1
 STAGES = (
     (4, 4, 4, 4),
-    (7, 7, 6, 6),
-    (12, 10, 9, 10),
-    (15, 13, 12, 12),
-    (17, 15, 14, 15),
-    (19, 18, 17, 17),
-    (21, 19, 18, 19),
-    (23, 22, 21, 22),
+    (8, 6, 5, 6),
+    (13, 10, 9, 10),
+    (15, 12, 12, 12),
+    (18, 15, 15, 15),
+    (20, 17, 17, 17),
+    (22, 20, 20, 20),
 )
 
 
@@ -177,6 +177,12 @@
         for peer in line:
             signal(tok_go, peer)
 
+    if nz > 1:
+
+        @pl.when(leader & (z == root))
+        def _():
+            all_groups()
+
     def cx_copy(h):
         cols = slice(h * 256, h * 256 + 256)
         return pltpu.make_async_remote_copy(
@@ -232,10 +238,12 @@
             tx_part(q, False).start()
             tx_part(q, True).start()
 
-        @pl.loop(1, CHIPS - 1)
-        def _(k):
-            tx_whole(k, False).start()
-            tx_whole(k, True).start()
+    def tx_next(*blocks):
+        @pl.when(is_end)
+        def _():
+            for k in blocks:
+                tx_whole(k, False).start()
+                tx_whole(k, True).start()
 
     sc_copy = pltpu.make_async_remote_copy(
         cot,
@@ -286,19 +294,15 @@
 
     def z_gather(k, zz):
         ref = gath.at[x, y, zz]
-        return stage_copy(4, k, ref, ref, z_next[k])
-
-    def z_pass(k, zz):
-        ref = gath.at[x, y, zz, half[k]]
-        return stage_copy(5, k, ref, ref, z_next[k])
+        return stage_copy(4, k, ref, ref, at_z(lax.rem(z + k + 1, nz)))
 
     def y_gather(k, yy):
         ref = gath.at[x, yy]
-        return stage_copy(6, k, ref, ref, y_peers[k])
+        return stage_copy(5, k, ref, ref, y_peers[k])
 
     def x_gather(k, xx):
         ref = gath.at[xx]
-        return stage_copy(7, k, ref, ref, x_peers[k])
+        return stage_copy(6, k, ref, ref, x_peers[k])
 
     @pl.when(is_next)
     def _():
@@ -346,12 +350,12 @@
 
     def up_copy(n):
         return pltpu.make_async_remote_copy(
-            up_buf.at[n], up_buf.at[n], up_send.at[n // NC], up_recv.at[n], device_id=above, device_id_type=MESH
+            up_buf.at[n], up_buf.at[n], up_send.at[n], up_recv.at[n], device_id=above, device_id_type=MESH
         )
 
     def dn_copy(n):
         return pltpu.make_async_remote_copy(
-            dn_buf.at[n], dn_buf.at[n], dn_send.at[n // NC], dn_recv.at[n], device_id=below, device_id_type=MESH
+            dn_buf.at[n], dn_buf.at[n], dn_send.at[n], dn_recv.at[n], device_id=below, device_id_type=MESH
         )
 
     def due(stage, t):
@@ -385,6 +389,11 @@
 
             up_copy(n).start()
 
+            @pl.when(su >= DEPTH)
+            def _():
+                before = su - DEPTH
+                up_copy((CHIPS - 1 - before // NC) * NC + lax.rem(before, NC)).wait_send()
+
         sd = t - (CHIPS - 2 - i) * LAG
         kd = sd // NC
 
@@ -404,6 +413,10 @@
                 dn_buf[n] = acc[...].astype(BF16)
 
             dn_copy(n).start()
+
+            @pl.when(sd >= DEPTH)
+            def _():
+                dn_copy(sd - DEPTH).wait_send()
 
         @pl.when(t == DECODE)
         def _():
@@ -433,10 +446,11 @@
 
             for k in range(nx - 1):
                 x_sum(k).start()
+            tx_next(1, 2)
 
             if nz > 1:
 
-                @pl.when(leader)
+                @pl.when(leader & (z != root))
                 def _():
                     all_groups()
 
@@ -454,6 +468,7 @@
 
             for k in range(ny - 1):
                 y_sum(k).start()
+            tx_next(3)
 
         @pl.when(due(1, t))
         def _():
@@ -473,6 +488,7 @@
 
                 for k in range(2):
                     z_far(k).start()
+            tx_next(4)
 
         @pl.when(due(2, t))
         def _():
@@ -483,6 +499,7 @@
                     part3[to, half[k]] += far3[k]
                 for k in range(2):
                     z_sum(k).start()
+            tx_next(5)
 
         @pl.when(due(3, t))
         def _():
@@ -500,36 +517,27 @@
             own = jnp.where(lax.rem(r, 2) == 0, own[0:8], own[8:16])
             own_p = jnp.concatenate([own[:, b * 128 : (b + 1) * 128] for b in range(4)], axis=0)
             gath[x, y, z] = (own_p - 0.7 * (0.9 * mom_next + average)).astype(BF16)
-            if nz > 1:
-                for k in range(2):
-                    z_gather(k, z).start()
+            for k in range(nz - 1):
+                z_gather(k, z).start()
+            tx_next(6)
             for b in range(4):
                 mn_v[:, b * 128 : (b + 1) * 128] = mom_next[8 * b : 8 * b + 8]
 
         @pl.when(due(4, t))
         def _():
-            if nz > 1:
-                for k in range(2):
-                    before = lax.rem(z + (nz - 1, 1)[k], nz)
-                    z_gather(k, before).wait_recv()
-                    z_pass(k, before).start()
-
-        @pl.when(due(5, t))
-        def _():
-            if nz > 1:
-                for k in range(2):
-                    z_pass(k, lax.rem(z + 2, nz)).wait_recv()
+            for k in range(nz - 1):
+                z_gather(k, lax.rem(z + nz - k - 1, nz)).wait_recv()
             for k in range(ny - 1):
                 y_gather(k, y).start()
 
-        @pl.when(due(6, t))
+        @pl.when(due(5, t))
         def _():
             for k in range(ny - 1):
                 y_gather(k, lax.rem(y + ny - k - 1, ny)).wait_recv()
             for k in range(nx - 1):
                 x_gather(k, x).start()
 
-        @pl.when(due(7, t))
+        @pl.when(due(6, t))
         def _():
             for k in range(nx - 1):
                 x_gather(k, lax.rem(x + nx - k - 1, nx)).wait_recv()
@@ -588,19 +596,12 @@
             whole = t_ext.at[0:TOK, 0 : (CHIPS - 1) * BLK]
             pltpu.make_async_copy(whole, whole, tx_send.at[other]).wait()
 
-    def wait_block(buf, sem, d):
-        whole = buf.at[pl.ds(d * NC, NC)]
-        pltpu.make_async_copy(whole, whole, sem.at[d]).wait()
-
-    @pl.loop(0, CHIPS)
-    def _(d):
-        @pl.when((i >= 1) & (d > i))
-        def _():
-            wait_block(up_buf, up_send, d)
-
-        @pl.when((i <= CHIPS - 2) & (d < i))
-        def _():
-            wait_block(dn_buf, dn_send, d)
+    for k in range(NC - DEPTH, NC):
+
+        @pl.when((i >= 1) & (i < CHIPS - 1))
+        def _(k=k):
+            up_copy((i + 1) * NC + k).wait_send()
+            dn_copy((i - 1) * NC + k).wait_send()
 
     for k in range(nx - 1):
         x_sum(k).wait_send()
@@ -612,8 +613,8 @@
         for k in range(2):
             z_far(k).wait_send()
             z_sum(k).wait_send()
-            z_gather(k, z).wait_send()
-            z_pass(k, lax.rem(z + (nz - 1, 1)[k], nz)).wait_send()
+    for k in range(nz - 1):
+        z_gather(k, z).wait_send()
 
 
 def store(a, b, c, a_out, b_out, c_out, sems):
@@ -668,12 +669,12 @@
             sem((4,)),
             sem((2,)),
             sem((NQ + CHIPS - 2, 2)),
-            sem((CHIPS,)),
             sem((CHIPS * NC,)),
-            sem((CHIPS,)),
             sem((CHIPS * NC,)),
-            sem((8, 3)),
-            sem((8, 3)),
+            sem((CHIPS * NC,)),
+            sem((CHIPS * NC,)),
+            sem((7, 3)),
+            sem((7, 3)),
             pltpu.SemaphoreType.REGULAR,
         ],
         compiler_params=pltpu.CompilerParams(

time: 111 us -> 103 us (0.928)
  the two profiles are of different devices: /device:TPU:4 before, /device:TPU:416 now
where the time goes in v3:
time: 103 us
  Pallas kernels  102 us (99%)
    pallas_call x1, Pallas kernels, body(): pl.pallas_call(functools.partial(kernel, dims, replicas), out_shape=(pltp...  101 us

profile of v3, /device:TPU:416, one launch (start us, length us, event | category | flops | bytes accessed | tf_op | source)
XLA Modules:
  0.0 102.7 jit_solution(5302930852374173053)
XLA Ops:
  0.6 101.1 %shard_map.85 = (bf16[512,512]{1,0:T(8,128)(2,1)S(1)}, bf16[512,512]{1,0:T(8,128)(2,1)S(1)}, f32[8,512]{1,0:T(8,128)S(1)}) custom-call(bf16[128,8192]{1,0:T(8,128)(2,1)} %tok.1, bf16[128,512]{1,0:T(8,128)(2,1)} %cot.1, bf16[512,512]{1,0:T(8,128)(2,1)} %bitcast.5, bf16[512,512]{1,0:T(8,128)(2,1)} %glob.1, f32[8,512]{1,0:T(8,128)} %mom.1, s32[4,16]{1,0:T(4,128)} %bitcast.6), custom_call_target="tpu_custom_call" | custom-call | tf_op jit(solution)/shard_map/pallas_call | solution.py:636
  101.7 1.0 shard_map.86

commit v4 on v3

--- a/solution.py
+++ b/solution.py
@@ -24,12 +24,12 @@
 DEPTH = 1
 STAGES = (
     (4, 4, 4, 4),
-    (8, 6, 5, 6),
-    (13, 10, 9, 10),
+    (8, 6, 6, 6),
+    (12, 9, 9, 9),
     (15, 12, 12, 12),
-    (18, 15, 15, 15),
-    (20, 17, 17, 17),
-    (22, 20, 20, 20),
+    (18, 16, 15, 16),
+    (20, 18, 17, 18),
+    (23, 21, 20, 21),
 )
 
 

time: 103 us -> 101 us (0.981)
  the two profiles are of different devices: /device:TPU:416 before, /device:TPU:65 now
where the time goes in v4:
time: 101 us
  Pallas kernels  101 us (100%)
    pallas_call x1, Pallas kernels, body(): pl.pallas_call(functools.partial(kernel, dims, replicas), out_shape=(pltp...  99.6 us

profile of v4, /device:TPU:65, one launch (start us, length us, event | category | flops | bytes accessed | tf_op | source)
XLA Modules:
  0.0 101.2 jit_solution(17533516902928929113)
XLA Ops:
  0.6 99.6 %shard_map.85 = (bf16[512,512]{1,0:T(8,128)(2,1)S(1)}, bf16[512,512]{1,0:T(8,128)(2,1)S(1)}, f32[8,512]{1,0:T(8,128)S(1)}) custom-call(bf16[128,8192]{1,0:T(8,128)(2,1)} %tok.1, bf16[128,512]{1,0:T(8,128)(2,1)} %cot.1, bf16[512,512]{1,0:T(8,128)(2,1)} %bitcast.5, bf16[512,512]{1,0:T(8,128)(2,1)} %glob.1, f32[8,512]{1,0:T(8,128)} %mom.1, s32[4,16]{1,0:T(4,128)} %bitcast.6), custom_call_target="tpu_custom_call" | custom-call | tf_op jit(solution)/shard_map/pallas_call | solution.py:636
  100.2 1.0 shard_map.86
